TPU v7x, 512 devices: a whole 4x8x8 slice. The times are simulated.
512 devices in a mesh: leaf: 128 (over y, z, core), vec: 4 (over x).
Axes of the slice: x: 4, y: 8, z: 8, core: 2. Of those that a mesh axis runs over, the one named last changes fastest.
Arguments:
- vectors: bfloat16 [64, 131072], P('vec', 'leaf'), may hold values from -6 to 6
- leaf_basis: bfloat16 [64, 131072], P(None, 'leaf'), may hold values from -0.75 to 0.75
- local_transfer: bfloat16 [64, 245760], P(None, 'leaf'), may hold values from -0.625 to 0.625
- upper_transfer: bfloat16 [64, 15872], replicated, may hold values from -0.625 to 0.625
- upper_coupling: bfloat16 [64, 256], replicated, may hold values from -0.75 to 0.75
- leaf_coupling: bfloat16 [64, 786432], P(None, 'leaf'), may hold values from -0.3125 to 0.3125
- far_list: int32 [6, 2048], P(None, 'leaf'), may hold values from 0 to 2047, as said below
- near_list: int32 [6, 2048], P(None, 'leaf'), may hold values from 0 to 2047, as said below
- near_tiles: bfloat16 [2048, 64, 384], P(('leaf', 'vec')), may hold values from -0.3125 to 0.3125
Outputs:
- product: bfloat16 [64, 131072], P('vec', 'leaf')
Inputs may be any that keep to these rules, and one draw needn't show every extreme that they name: `far_list`: every entry names a leaf 2 to 16 leaves away from its own leaf l (column l); on every device some leaf has an entry exactly 16 leaves away. `near_list`: row 0 names the leaf itself; every other entry names a leaf 1 to 16 leaves away from its own leaf; on every device some leaf has an entry exactly 16 leaves away.
All inputs are finite; a program needn't handle non-finite values.
Results may differ from a plain program's by a relative error of at most 0.0055.
Values may be sent and summed in bfloat16 or wider, within the bound.
A program may use at most 64 MiB of HBM per device.

v0:
```python
import jax
import jax.numpy as jnp
from jax import lax
from jax.experimental import pallas as pl
from jax.experimental.pallas import tpu as pltpu
from jax.sharding import PartitionSpec as P

MESH = pl.DeviceIdType.MESH
BF = jnp.bfloat16
F32 = jnp.float32
ROW = 16
ROWS = 8
LEAF_COUNT = ROW * ROWS
BASES = (0, 16, 24, 28, 30)
PREV = 42
NEXT = 51


def low(shape):
    return lax.broadcasted_iota(jnp.int32, shape, 1) < 64


def halves(a, b):
    return jnp.where(low(a.shape), a, b)


def turned(tile):
    return pltpu.roll(tile, 64, 1)


def rounded(x):
    return x.astype(BF).astype(F32)


def hilo(x):
    hi = rounded(x)
    return halves(hi, x - hi).astype(BF)


def two_terms(x):
    hi = rounded(x)
    return hi.astype(BF), (x - hi).astype(BF)


def nn(a, b):
    return jnp.dot(a, b, preferred_element_type=F32)


def nt(a, b):
    return lax.dot_general(a, b, (((1,), (1,)), ((), ())), preferred_element_type=F32)


def tn(a, b):
    return lax.dot_general(a, b, (((0,), (0,)), ((), ())), preferred_element_type=F32)


def diagonal(block):
    none = jnp.zeros_like(block)
    return rows(halves(block, none), halves(none, block))


def rows(*parts):
    return jnp.concatenate(parts, axis=0)


def lanes(*parts):
    return jnp.concatenate(parts, axis=1)


def kernel(
    vec_h, basis_h, lt_h, ut_h, uc_h, lc_h, far_h, near_h, tiles_h, out_ref,
    basis_v, lt_v, ut_v, uc_v, lc_v, far_s, near_s, tiles_v,
    arrived, points, coeffs, root_tile, nodes, heads, tails,
    dup, path_hi, path_lo, r0_hi, r0_lo, to_points, lifted_couplings, from_top, from_row, far_out, near_out, near_in,
    in_sem, send_sem, recv_sem, flag_0, flag_1,
):
    d = lax.axis_index("leaf")
    x = lax.axis_index("vec")
    y = d >> 4
    i = d & 15
    z = i >> 1
    c = i & 1

    def load(src, dst, n):
        copy = pltpu.make_async_copy(src, dst, in_sem.at[n])
        copy.start()
        return copy

    own = pl.ds(pl.multiple_of(16 * x, 16), 16)
    vec_in = load(vec_h, arrived.at[1, own], 0)
    basis_in = load(basis_h, basis_v, 1)
    lt_in = load(lt_h, lt_v, 2)

    right = (d + 1) & (LEAF_COUNT - 1)
    left = (d + LEAF_COUNT - 1) & (LEAF_COUNT - 1)
    sibling = d + 1 - 2 * c
    column_peers = [(d + ROW * k) & (LEAF_COUNT - 1) for k in (4, 3, 5, 2, 1, 6, 7)]
    vec_peers = [(x + k) & 3 for k in (2, 1, 3)]

    barrier = pltpu.get_barrier_semaphore()

    def announce(leaf, vec):
        pl.semaphore_signal(barrier, inc=1, device_id={"leaf": leaf, "vec": vec}, device_id_type=MESH)

    @pl.when(z < 4)
    def _():
        for k in range(1, 8):
            announce(ROW * y + 2 * ((z + k) & 7), x)

    @pl.when(z >= 4)
    def _():
        for k in range(1, 8):
            announce(ROW * y + 2 * ((z + k) & 7) + 1, x)

    announce(sibling, x)
    near_start = z < 4
    announce((d + jnp.where(c == 0, LEAF_COUNT - 2 + (z >> 2), jnp.where(z == 7, 2, 1))) & (LEAF_COUNT - 1), x)
    for peer in vec_peers:
        announce(d - c + (z >> 2), peer)
    for peer in column_peers:
        announce(peer - c + 1, x)

    ends = jnp.where(jnp.logical_or(z == 0, z == 3), 1, 0)
    last = jnp.where(z == 7, 1, 0)
    count_0 = jnp.where(near_start, 15 - ends, 10 + last)
    count_1 = jnp.where(near_start, 23 + ends, 28 - last)

    def tell(flag):
        pl.semaphore_signal(flag, inc=1, device_id={"leaf": sibling, "vec": x}, device_id_type=MESH)

    @pl.when(jnp.logical_and(c == 0, z == 7))
    def _():
        pl.semaphore_wait(barrier, count_0)
        tell(flag_0)

    ut_in = [
        load(ut_h.at[:, pl.ds(pl.multiple_of(1024 * y, 128), 1024)], ut_v.at[:, 0:1024], 3),
        load(ut_h.at[:, pl.ds(pl.multiple_of(8192 + 512 * y, 128), 512)], ut_v.at[:, 1024:1536], 4),
        load(ut_h.at[:, pl.ds(pl.multiple_of(12288 + 256 * y, 128), 256)], ut_v.at[:, 1536:1792], 5),
        load(ut_h.at[:, pl.ds(pl.multiple_of(14336 + 128 * y, 128), 128)], ut_v.at[:, 1792:1920], 6),
        load(ut_h.at[:, 15360:15872], ut_v.at[:, 1920:2432], 7),
    ]

    def send(src, dst, n_send, n_recv, leaf, vec):
        copy = pltpu.make_async_remote_copy(
            src_ref=src, dst_ref=dst, send_sem=send_sem.at[n_send], recv_sem=recv_sem.at[n_recv],
            device_id={"leaf": leaf, "vec": vec}, device_id_type=MESH,
        )
        copy.start()
        return copy

    def wait_for(ref, sem):
        pltpu.make_async_copy(ref, ref, sem).wait()

    def send_root(t):
        send(root_tile, nodes.at[i], 1, 1, ROW * y + t, x)

    def to_vec_peers():
        for peer in vec_peers:
            send(vec_h, arrived.at[1, own], 0, 0, d, peer)

    def far_right():
        send(coeffs.at[8:16, 0], coeffs.at[0:8, 0], 2, 2, right, x)

    def far_left():
        send(coeffs.at[8:16, 0], coeffs.at[16:24, 0], 3, 3, left, x)

    def near_right():
        send(arrived.at[1], arrived.at[0], 4, 4, right, x)

    def near_left():
        send(arrived.at[1], arrived.at[2], 5, 5, left, x)

    row_end = jnp.logical_and(c == 1, z == 7)
    row_start = jnp.logical_and(c == 0, z == 0)
    left_now = jnp.logical_and(near_start, jnp.logical_or(c == 1, z > 0))
    right_now = jnp.logical_and(near_start, jnp.logical_or(c == 0, z < 3))
    left_later = jnp.logical_not(jnp.logical_or(left_now, row_start))
    right_later = jnp.logical_not(jnp.logical_or(right_now, row_end))

    vec_in.wait()
    basis_in.wait()
    lt_in.wait()

    def local_top():
        transfer = lt_v[:, 1792:1920]
        crossed = turned(transfer)
        return halves(transfer, crossed), halves(crossed, transfer)

    top = local_top()

    group = lax.broadcasted_iota(jnp.int32, (16, 256), 1) >> 6
    zero = jnp.zeros((16, 256), BF)

    def paired(product):
        return [
            halves(product[0:16, 0:128], product[16:32, 0:128]),
            halves(product[32:48, 128:256], product[48:64, 128:256]),
        ]

    leaves = []
    for q in range(4):
        tile = arrived[1, own, 256 * q : 256 * q + 256]
        block = basis_v[:, 256 * q : 256 * q + 256]
        spread = rows(*[jnp.where(group == e, tile, zero) for e in range(4)])
        leaves.append(nt(spread, rows(block, block)))
    for j in range(8):
        pair = leaves[j // 2][32 * (j % 2) : 32 * (j % 2) + 32]
        coeffs[8 + j, 0] = halves(pair[0:16], pair[16:32]).astype(BF)
        coeffs[8 + j, 1] = halves(pair[16:32], pair[0:16]).astype(BF)

    @pl.when(row_end)
    def _():
        pl.semaphore_wait(flag_0, 1)
        send(vec_h, arrived.at[0, own], 10, 4, right, x)
        far_right()

    current = []
    for q in range(4):
        transfer = lt_v[:, 256 * q : 256 * q + 256]
        current += paired(nn(hilo(leaves[q]), rows(transfer, transfer)))
    for start in (1024, 1536):
        following = []
        for q in range(len(current) // 4):
            hi, lo = two_terms(rows(*current[4 * q : 4 * q + 4]))
            transfer = lt_v[:, start + 256 * q : start + 256 * q + 256]
            following += paired(nn(lanes(hi, lo), rows(transfer, transfer, transfer, transfer)))
        current = following
    first_hi, first_lo = two_terms(current[0])
    second_hi, second_lo = two_terms(current[1])
    root = nn(lanes(first_hi, first_lo, second_hi, second_lo), rows(*([top[0]] * 4 + [top[1]] * 4)))
    root_tile[...] = hilo(root)
    nodes[i] = root_tile[...]

    late_loads = [
        pltpu.make_async_copy(src, dst, in_sem.at[8 + n])
        for n, (src, dst) in enumerate(
            ((uc_h, uc_v), (lc_h, lc_v), (far_h, far_s), (near_h, near_s), (tiles_h, tiles_v))
        )
    ]
    uc_in, lc_in, far_in_s, near_in_s, tiles_in = late_loads

    def roots_out():
        @pl.when(jnp.logical_and(c == 0, z < 7))
        def _():
            pl.semaphore_wait(barrier, count_0)
            tell(flag_0)

        @pl.when(jnp.logical_and(c == 1, z < 7))
        def _():
            pl.semaphore_wait(flag_0, 1)

        for k in range(1, 8):
            send_root((i + k) & 7)

        @pl.when(z >= 4)
        def _():
            send_root(i & 7)

        @pl.when(near_start)
        def _():
            to_vec_peers()

        @pl.when(left_now)
        def _():
            far_left()

        @pl.when(right_now)
        def _():
            far_right()

        for copy in late_loads:
            copy.start()

    def matrices():
        for copy in ut_in:
            copy.wait()
        for p in range(19):
            pair = ut_v[:, 128 * p : 128 * p + 128]
            swapped = turned(pair)
            dup[2 * p] = halves(pair, swapped)
            dup[2 * p + 1] = halves(swapped, pair)

        path = dup[i]
        path_hi[0] = path
        path = path.astype(F32)
        below = local_top()
        below = [(below[0], None), (below[1], None)]
        row_below = [(dup[28], None), (dup[29], None)]

        def path_step(path, u):
            matrix = dup[BASES[u] + (i >> u if u < 4 else y)]
            path = nn(hilo(path), rows(matrix, matrix))
            path_hi[u], path_lo[u] = two_terms(path)
            return path

        def product_step(below, transfers, start):
            following = []
            for m, (hi, lo) in enumerate(below):
                left_side = diagonal(transfers[:, start + 128 * m : start + 128 * m + 128])
                if lo is None:
                    product = nn(left_side, rows(hi, hi))
                else:
                    product = nn(lanes(left_side, left_side), rows(hi, hi, lo, lo))
                hi, lo = two_terms(product)
                following += [(hi[0:64], lo[0:64]), (hi[64:128], lo[64:128])]
            return following

        for u, start in ((1, 1536), (2, 1024), (3, 0)):
            path = path_step(path, u)
            below = product_step(below, lt_v, start)
            row_below = product_step(row_below, ut_v, start)
        path_step(path, 4)
        for m in range(8):
            r0_hi[m] = rows(below[2 * m][0], below[2 * m + 1][0])
            r0_lo[m] = rows(below[2 * m][1], below[2 * m + 1][1])
        for m, (hi, lo) in enumerate(row_below):
            from_row[0, m] = rows(hi, hi)
            from_row[1, m] = rows(lo, lo)

    def turn(n, carry):
        @pl.when(n == (z >> 2))
        def _():
            matrices()

        @pl.when(n == 0)
        def _():
            roots_out()

        return carry

    lax.fori_loop(0, 2, turn, 0)

    def fold(j, carry):
        at = pl.ds(pl.multiple_of(128 * j, 128), 128)
        block = diagonal(basis_v[:, at])
        hi, lo = two_terms(tn(r0_hi[j], block) + tn(r0_lo[j], block))
        to_points[0:128, at] = hi
        to_points[128:256, at] = lo
        return carry

    lax.fori_loop(0, 8, fold, 0, unroll=2)

    @pl.when(near_start)
    def _():
        wait_for(arrived.at[1, 0:48], recv_sem.at[0])

    @pl.when(left_now)
    def _():
        near_left()

    @pl.when(right_now)
    def _():
        near_right()

    uc_in.wait()
    couplings = rows(uc_v[...], uc_v[...])
    for e in range(2):
        value = nn(halves(path_hi[3 + e], path_lo[3 + e]), couplings)
        value = jnp.transpose(rows(value, value))
        for o in range(4):
            lifted_couplings[e, o] = value[64 * o : 64 * o + 64]

    def slot(offset, odd):
        index = jnp.where(offset == -3, 0, jnp.where(offset == -2, 1, jnp.where(offset == 2, 2, 3)))
        wide = jnp.logical_or(
            jnp.logical_and(offset == -3, odd == 1), jnp.logical_and(offset == 3, odd == 0)
        )
        valid = jnp.logical_or(jnp.logical_or(offset == -2, offset == 2), wide)
        return index, jnp.where(valid, 1.0, 0.0).astype(F32)

    def gather_top(n, carry):
        index, keep = slot(n - y, y & 1)
        value = lifted_couplings[0, index] * keep
        index, keep = slot((n >> 1) - (y >> 1), (y >> 1) & 1)
        hi, lo = two_terms(lifted_couplings[1, index] * keep)
        hi, lo = two_terms(value + nn(dup[30 + n], rows(hi, lo)))
        from_top[0, n] = rows(hi, hi)
        from_top[1, n] = rows(lo, lo)
        return carry

    lax.fori_loop(0, 8, gather_top, 0, unroll=4)

    def fill(w):
        def step(j, carry):
            block = arrived[w, :, pl.ds(pl.multiple_of(128 * j, 128), 128)]
            points[8 * w + j, 0] = block
            points[8 * w + j, 1] = turned(block)
            return carry

        lax.fori_loop(0, 8, step, 0, unroll=2)

    @pl.when(c == 1)
    def _():
        pl.semaphore_wait(barrier, count_1)
        tell(flag_1)

    @pl.when(c == 0)
    def _():
        pl.semaphore_wait(flag_1, 1)

    for k in range(1, 8):
        send_root(8 + ((i + k) & 7))

    @pl.when(z < 4)
    def _():
        send_root(8 + i)

    @pl.when(z >= 4)
    def _():
        to_vec_peers()

    @pl.when(jnp.logical_not(left_now))
    def _():
        far_left()

    @pl.when(right_later)
    def _():
        far_right()

    @pl.when(z >= 4)
    def _():
        wait_for(arrived.at[1, 0:48], recv_sem.at[0])

    @pl.when(row_start)
    def _():
        send(vec_h, arrived.at[2, own], 11, 5, left, x)

    @pl.when(left_later)
    def _():
        near_left()

    @pl.when(right_later)
    def _():
        near_right()

    fill(1)

    first_leaf = ROW * d - ROW

    def chosen(table, lists, slots, column):
        parts = []
        for s in range(0, slots, 2):
            a = jnp.clip(lists[s, column] - first_leaf, 0, 3 * ROW - 1)
            b = jnp.clip(lists[s + 1, column] - first_leaf, 0, 3 * ROW - 1)
            parts.append(halves(table[a >> 1, a & 1], table[b >> 1, 1 - (b & 1)]))
        return lanes(*parts)

    def far_part():
        far_in_s.wait()
        lc_in.wait()
        wait_for(coeffs.at[0:8, 0], recv_sem.at[2])
        wait_for(coeffs.at[16:24, 0], recv_sem.at[3])
        for p in list(range(8)) + list(range(16, 24)):
            coeffs[p, 1] = turned(coeffs[p, 0])
        for j in range(8):
            source = rows(*[chosen(coeffs, far_s, 6, 2 * j + e) for e in range(2)])
            value = nt(source, rows(lc_v[:, 768 * j : 768 * j + 384], lc_v[:, 768 * j + 384 : 768 * j + 768]))
            hi, lo = two_terms(halves(value[0:16], value[16:32]))
            block = diagonal(basis_v[:, 128 * j : 128 * j + 128])
            far_out[j] = nn(lanes(hi, lo), rows(block, block))

    def near_part():
        near_in_s.wait()
        tiles_in.wait()

        @pl.when(row_start)
        def _():
            wait_for(arrived.at[0, 0:48], recv_sem.at[10])

        @pl.when(jnp.logical_not(row_start))
        def _():
            wait_for(arrived.at[0], recv_sem.at[4])

        @pl.when(row_end)
        def _():
            wait_for(arrived.at[2, 0:48], recv_sem.at[11])

        @pl.when(jnp.logical_not(row_end))
        def _():
            wait_for(arrived.at[2], recv_sem.at[5])

        fill(0)
        fill(2)
        for q in range(2):
            source = rows(*[chosen(points, near_s, 6, 4 * x + 2 * q + e) for e in range(2)])
            value = nt(source, rows(tiles_v[2 * q], tiles_v[2 * q + 1]))
            value = halves(value[0:64], value[64:128]).astype(BF)
            for v in range(4):
                near_out[v, q] = value[16 * v : 16 * v + 16]
        for n, peer in enumerate(vec_peers):
            send(near_out.at[peer], near_in.at[x], 9, 9, d, peer)
        near_in[x] = near_out[x]

    @pl.when(row_start)
    def _():
        wait_for(arrived.at[0, 0:16], recv_sem.at[4])
        for peer in vec_peers:
            send(arrived.at[0, own], arrived.at[0, own], 10, 10, d, peer)

    def row_tree():
        wait_for(nodes.at[0:15], recv_sem.at[1])

        @pl.when(row_end)
        def _():
            wait_for(arrived.at[2, 0:16], recv_sem.at[5])
            for peer in vec_peers:
                send(arrived.at[2, own], arrived.at[2, own], 11, 11, d, peer)

        roots = lanes(*[nodes[m] for m in range(ROW)])
        top_tile = hilo(nn(roots, from_row[0].reshape(2048, 128)) + nn(roots, from_row[1].reshape(2048, 128)))
        nodes[30 + y] = top_tile
        heads[8] = top_tile
        tails[8] = top_tile
        for peer in column_peers[:4] + column_peers[5:6]:
            send(nodes.at[30 + y], nodes.at[30 + y], 8, 8, peer, x)
        for u in range(3):
            base, count = BASES[u], ROW >> u
            for m in range(count // 2):
                left_m, right_m = dup[base + 2 * m], dup[base + 2 * m + 1]
                value = nn(lanes(nodes[base + 2 * m], nodes[base + 2 * m + 1]), rows(left_m, left_m, right_m, right_m))
                nodes[BASES[u + 1] + m] = hilo(value)
        for u in range(4):
            for e in range(2):
                heads[2 * u + e] = nodes[BASES[u] + e]
                tails[2 * u + e] = nodes[BASES[u + 1] - 2 + e]
        send(tails, nodes.at[PREV : PREV + 9], 6, 6, column_peers[4], x)
        send(heads, nodes.at[NEXT : NEXT + 9], 7, 7, column_peers[6], x)

    row_tree()
    near_part()
    far_part()

    weights = []
    for o in range(2):
        pair = uc_v[:, 128 * o : 128 * o + 128]
        swapped = turned(pair)
        weights += [halves(pair, swapped), halves(swapped, pair)]
    weights = lanes(*weights)
    wait_for(nodes.at[0:9], recv_sem.at[6])
    wait_for(nodes.at[0:9], recv_sem.at[7])
    sources = []
    for u in range(4):
        g = d >> u
        odd = g & 1
        number = LEAF_COUNT >> u
        count = ROW >> u
        parts = []
        for o, wanted in ((-3, odd == 1), (-2, None), (2, None), (3, odd == 0)):
            shift = o if wanted is None else (-3 * odd if o < 0 else 3 * (1 - odd))
            place = (i >> u) + shift
            place = jnp.where(
                place < 0,
                PREV + 2 + 2 * u + place,
                jnp.where(place < count, BASES[u] + place, NEXT + 2 * u - count + place),
            )
            valid = (g + o >= 0) if o < 0 else (g + o < number)
            if wanted is not None:
                valid = jnp.logical_and(valid, wanted)
            keep = jnp.where(valid, 1.0, 0.0).astype(F32)
            parts.append((nodes[place].astype(F32) * keep).astype(BF))
        sources.append(lanes(*parts))
    coupled = nt(rows(*sources), rows(weights, weights))
    left_side, right_side = [], []
    for u in range(1, 4):
        tile = hilo(coupled[16 * u : 16 * u + 16])
        left_side.append(tile)
        right_side.append(path_hi[u - 1])
        if u > 1:
            left_side.append(tile)
            right_side.append(path_lo[u - 1])
    matrix = lanes(*right_side)
    down = coupled[0:16] + nt(lanes(*left_side), rows(matrix, matrix))

    nodes[30 + ((y + 7) & 7)] = nodes[PREV + 8]
    nodes[30 + ((y + 1) & 7)] = nodes[NEXT + 8]
    wait_for(nodes.at[0:5], recv_sem.at[8])
    tops = lanes(*[nodes[30 + n] for n in range(8)])
    down = down + nn(tops, from_top[0].reshape(1024, 128)) + nn(tops, from_top[1].reshape(1024, 128))
    down = hilo(down)
    value = nn(lanes(down, down), to_points[...])
    wait_for(near_in.at[0:3], recv_sem.at[9])
    for j in range(8):
        at = slice(128 * j, 128 * j + 128)
        out_ref[:, at] = (value[:, at] + far_out[j] + near_in[j // 2, j % 2].astype(F32)).astype(BF)

    wait_for(arrived.at[1, 0:48], send_sem.at[0])
    wait_for(nodes.at[0:15], send_sem.at[1])
    wait_for(coeffs.at[0:8, 0], send_sem.at[2])
    wait_for(coeffs.at[0:8, 0], send_sem.at[3])

    @pl.when(row_end)
    def _():
        wait_for(arrived.at[0, 0:16], send_sem.at[10])
        wait_for(arrived.at[2, 0:48], send_sem.at[11])

    @pl.when(row_start)
    def _():
        wait_for(arrived.at[0, 0:48], send_sem.at[10])
        wait_for(arrived.at[2, 0:16], send_sem.at[11])

    @pl.when(jnp.logical_not(row_end))
    def _():
        wait_for(arrived.at[0], send_sem.at[4])

    @pl.when(jnp.logical_not(row_start))
    def _():
        wait_for(arrived.at[2], send_sem.at[5])

    wait_for(nodes.at[0:9], send_sem.at[6])
    wait_for(nodes.at[0:9], send_sem.at[7])
    wait_for(nodes.at[0:5], send_sem.at[8])
    wait_for(near_out.at[0:3], send_sem.at[9])


def shards(vectors, leaf_basis, local_transfer, upper_transfer, upper_coupling, leaf_coupling, far_list, near_list, near_tiles):
    tile = (16, 128)
    scratch = [
        pltpu.VMEM(leaf_basis.shape, BF),
        pltpu.VMEM(local_transfer.shape, BF),
        pltpu.VMEM((64, 2432), BF),
        pltpu.VMEM(upper_coupling.shape, BF),
        pltpu.VMEM(leaf_coupling.shape, BF),
        pltpu.SMEM(far_list.shape, jnp.int32),
        pltpu.SMEM(near_list.shape, jnp.int32),
        pltpu.VMEM(near_tiles.shape, BF),
        pltpu.VMEM((3, 64, 1024), BF),
        pltpu.VMEM((24, 2, 64, 128), BF),
        pltpu.VMEM((24, 2) + tile, BF),
        pltpu.VMEM(tile, BF),
        pltpu.VMEM((60,) + tile, BF),
        pltpu.VMEM((9,) + tile, BF),
        pltpu.VMEM((9,) + tile, BF),
        pltpu.VMEM((38, 64, 128), BF),
        pltpu.VMEM((5, 64, 128), BF),
        pltpu.VMEM((5, 64, 128), BF),
        pltpu.VMEM((8, 128, 128), BF),
        pltpu.VMEM((8, 128, 128), BF),
        pltpu.VMEM((256, 1024), BF),
        pltpu.VMEM((2, 4, 64, 128), F32),
        pltpu.VMEM((2, 8, 128, 128), BF),
        pltpu.VMEM((2, ROW, 128, 128), BF),
        pltpu.VMEM((8,) + tile, F32),
        pltpu.VMEM((4, 2) + tile, BF),
        pltpu.VMEM((4, 2) + tile, BF),
        pltpu.SemaphoreType.DMA((13,)),
        pltpu.SemaphoreType.DMA((12,)),
        pltpu.SemaphoreType.DMA((12,)),
        pltpu.SemaphoreType.REGULAR,
        pltpu.SemaphoreType.REGULAR,
    ]
    return pl.pallas_call(
        kernel,
        out_shape=pltpu.VMEM(vectors.shape, BF),
        in_specs=[pl.BlockSpec(memory_space=pl.ANY)] * 9,
        out_specs=pl.BlockSpec(memory_space=pltpu.VMEM),
        scratch_shapes=scratch,
        compiler_params=pltpu.CompilerParams(
            collective_id=0, has_side_effects=True, vmem_limit_bytes=62 * 1024 * 1024
        ),
    )(vectors, leaf_basis, local_transfer, upper_transfer, upper_coupling, leaf_coupling, far_list, near_list, near_tiles)


def solution(mesh):
    placed = (
        P("vec", "leaf"),
        P(None, "leaf"),
        P(None, "leaf"),
        P(),
        P(),
        P(None, "leaf"),
        P(None, "leaf"),
        P(None, "leaf"),
        P(("leaf", "vec"), None, None),
    )
    return jax.shard_map(
        shards, mesh=mesh, in_specs=placed, out_specs=P("vec", "leaf"), check_vma=False
    )
```

profile of v0, /device:TPU:2, one launch (start us, length us, event | category | flops | bytes accessed | tf_op | source)
XLA Modules:
  0.0 24.4 jit_solution(3860596575314611597)
XLA Ops:
  0.0 23.8 %shard_map.91 = bf16[16,1024]{1,0:T(8,128)(2,1)S(1)} custom-call(bf16[16,1024]{1,0:T(8,128)(2,1)} %vec_h.1, bf16[64,1024]{1,0:T(8,128)(2,1)} %basis_h.1, bf16[64,1920]{1,0:T(8,128)(2,1)} %lt_h.1, bf16[64,15872]{1,0:T(8,128)(2,1)} %ut_h.1, bf16[64,256]{1,0:T(8,128)(2,1)} %uc_h.1, bf16[64,6144]{1,0:T(8,128)(2,1)} %lc_h.1, s32[6,16]{1,0:T(8,128)} %far_h.1, ...), custom_call_target="tpu_custom_call" | custom-call | tf_op jit(solution)/shard_map/pallas_call | solution.py:652
  23.8 0.6 %copy.11 = bf16[16,1024]{1,0:T(8,128)(2,1)} copy(bf16[16,1024]{1,0:T(8,128)(2,1)S(1)} %shard_map.91) | data formatting | bytes 65536
where the time goes:
time: 24.5 us; the launch traced here: 24.4 us
  Pallas kernels  23.8 us (97%)
  local copies, waits for them, and re-layouts  0.62 us (3%)
    pallas_call x1, Pallas kernels, shards(): pl.pallas_call(kernel, out_shape=pltpu.VMEM(vectors.shape, BF), in_specs=...  23.8 us
    unnamed x1, local copies, waits for them, and re-layouts  0.62 us

commit v1 on v0

--- a/solution.py
+++ b/solution.py
@@ -80,6 +80,8 @@
     i = d & 15
     z = i >> 1
     c = i & 1
+    row_end = jnp.logical_and(c == 1, z == 7)
+    row_start = jnp.logical_and(c == 0, z == 0)
 
     def load(src, dst, n):
         copy = pltpu.make_async_copy(src, dst, in_sem.at[n])
@@ -102,6 +104,26 @@
     def announce(leaf, vec):
         pl.semaphore_signal(barrier, inc=1, device_id={"leaf": leaf, "vec": vec}, device_id_type=MESH)
 
+    announce(sibling, x)
+    near_start = z < 4
+    ends = jnp.where(jnp.logical_or(z == 0, z == 3), 1, 0)
+    last = jnp.where(z == 7, 1, 0)
+    count_0 = jnp.where(near_start, 15 - ends, 10 + 4 * last)
+    count_1 = jnp.where(near_start, 23 + ends, 28 - last)
+
+    def tell(flag):
+        pl.semaphore_signal(flag, inc=1, device_id={"leaf": sibling, "vec": x}, device_id_type=MESH)
+
+    @pl.when(jnp.logical_and(c == 0, z == 7))
+    def _():
+        pl.semaphore_wait(barrier, count_0)
+        tell(flag_0)
+
+    @pl.when(row_start)
+    def _():
+        for peer in vec_peers:
+            announce((d + LEAF_COUNT - 2) & (LEAF_COUNT - 1), peer)
+
     @pl.when(z < 4)
     def _():
         for k in range(1, 8):
@@ -112,26 +134,12 @@
         for k in range(1, 8):
             announce(ROW * y + 2 * ((z + k) & 7) + 1, x)
 
-    announce(sibling, x)
-    near_start = z < 4
     announce((d + jnp.where(c == 0, LEAF_COUNT - 2 + (z >> 2), jnp.where(z == 7, 2, 1))) & (LEAF_COUNT - 1), x)
     for peer in vec_peers:
         announce(d - c + (z >> 2), peer)
     for peer in column_peers:
         announce(peer - c + 1, x)
 
-    ends = jnp.where(jnp.logical_or(z == 0, z == 3), 1, 0)
-    last = jnp.where(z == 7, 1, 0)
-    count_0 = jnp.where(near_start, 15 - ends, 10 + last)
-    count_1 = jnp.where(near_start, 23 + ends, 28 - last)
-
-    def tell(flag):
-        pl.semaphore_signal(flag, inc=1, device_id={"leaf": sibling, "vec": x}, device_id_type=MESH)
-
-    @pl.when(jnp.logical_and(c == 0, z == 7))
-    def _():
-        pl.semaphore_wait(barrier, count_0)
-        tell(flag_0)
 
     ut_in = [
         load(ut_h.at[:, pl.ds(pl.multiple_of(1024 * y, 128), 1024)], ut_v.at[:, 0:1024], 3),
@@ -171,12 +179,16 @@
     def near_left():
         send(arrived.at[1], arrived.at[2], 5, 5, left, x)
 
-    row_end = jnp.logical_and(c == 1, z == 7)
-    row_start = jnp.logical_and(c == 0, z == 0)
     left_now = jnp.logical_and(near_start, jnp.logical_or(c == 1, z > 0))
     right_now = jnp.logical_and(near_start, jnp.logical_or(c == 0, z < 3))
     left_later = jnp.logical_not(jnp.logical_or(left_now, row_start))
     right_later = jnp.logical_not(jnp.logical_or(right_now, row_end))
+
+    @pl.when(row_end)
+    def _():
+        pl.semaphore_wait(flag_0, 1)
+        for peer in [x] + vec_peers:
+            send(vec_h, arrived.at[0, own], 10, 4, right, peer)
 
     vec_in.wait()
     basis_in.wait()
@@ -211,8 +223,6 @@
 
     @pl.when(row_end)
     def _():
-        pl.semaphore_wait(flag_0, 1)
-        send(vec_h, arrived.at[0, own], 10, 4, right, x)
         far_right()
 
     current = []
@@ -463,14 +473,7 @@
     def near_part():
         near_in_s.wait()
         tiles_in.wait()
-
-        @pl.when(row_start)
-        def _():
-            wait_for(arrived.at[0, 0:48], recv_sem.at[10])
-
-        @pl.when(jnp.logical_not(row_start))
-        def _():
-            wait_for(arrived.at[0], recv_sem.at[4])
+        wait_for(arrived.at[0], recv_sem.at[4])
 
         @pl.when(row_end)
         def _():
@@ -491,12 +494,6 @@
         for n, peer in enumerate(vec_peers):
             send(near_out.at[peer], near_in.at[x], 9, 9, d, peer)
         near_in[x] = near_out[x]
-
-    @pl.when(row_start)
-    def _():
-        wait_for(arrived.at[0, 0:16], recv_sem.at[4])
-        for peer in vec_peers:
-            send(arrived.at[0, own], arrived.at[0, own], 10, 10, d, peer)
 
     def row_tree():
         wait_for(nodes.at[0:15], recv_sem.at[1])
@@ -591,12 +588,11 @@
 
     @pl.when(row_end)
     def _():
-        wait_for(arrived.at[0, 0:16], send_sem.at[10])
+        wait_for(arrived.at[0], send_sem.at[10])
         wait_for(arrived.at[2, 0:48], send_sem.at[11])
 
     @pl.when(row_start)
     def _():
-        wait_for(arrived.at[0, 0:48], send_sem.at[10])
         wait_for(arrived.at[2, 0:16], send_sem.at[11])
 
     @pl.when(jnp.logical_not(row_end))

time: 24.5 us -> 24 us (0.980)
  the two profiles are of different devices: /device:TPU:2 before, /device:TPU:1 now
where the time goes in v1:
time: 24 us; the launch traced here: 23.9 us
  Pallas kernels  23.3 us (97%)
  local copies, waits for them, and re-layouts  0.62 us (3%)
    pallas_call x1, Pallas kernels, shards(): pl.pallas_call(kernel, out_shape=pltpu.VMEM(vectors.shape, BF), in_specs=...  23.3 us
    unnamed x1, local copies, waits for them, and re-layouts  0.62 us

profile of v1, /device:TPU:1, one launch (start us, length us, event | category | flops | bytes accessed | tf_op | source)
XLA Modules:
  0.0 23.9 jit_solution(11348780355254394521)
XLA Ops:
  0.0 23.3 %shard_map.91 = bf16[16,1024]{1,0:T(8,128)(2,1)S(1)} custom-call(bf16[16,1024]{1,0:T(8,128)(2,1)} %vec_h.1, bf16[64,1024]{1,0:T(8,128)(2,1)} %basis_h.1, bf16[64,1920]{1,0:T(8,128)(2,1)} %lt_h.1, bf16[64,15872]{1,0:T(8,128)(2,1)} %ut_h.1, bf16[64,256]{1,0:T(8,128)(2,1)} %uc_h.1, bf16[64,6144]{1,0:T(8,128)(2,1)} %lc_h.1, s32[6,16]{1,0:T(8,128)} %far_h.1, ...), custom_call_target="tpu_custom_call" | custom-call | tf_op jit(solution)/shard_map/pallas_call | solution.py:648
  23.3 0.6 %copy.11 = bf16[16,1024]{1,0:T(8,128)(2,1)} copy(bf16[16,1024]{1,0:T(8,128)(2,1)S(1)} %shard_map.91) | data formatting | bytes 65536
